TPU v7x, 32 devices: a whole 2x2x4 slice. The times are simulated.
32 devices in a mesh: groups: 2 (over y), seq: 4 (over z), dp: 2 (over x), head: 2 (over core).
Axes of the slice: x: 2, y: 2, z: 4, core: 2. Of those that a mesh axis runs over, the one named last changes fastest.
Arguments:
- latents: bfloat16 [4, 8, 512, 1024], P(('groups', 'dp'), None, 'seq', 'head'), parts along dimension 0, may hold values from -6 to 6
- log_decay: bfloat16 [4, 8, 512, 8], P(('groups', 'dp'), None, 'seq', 'head'), parts along dimension 0, may hold values from -1 to 0, as said below
- seg_lengths: int32 [4, 4], P(('groups', 'dp')), parts along dimension 0, may hold values from 1 to 2048, 4096 in all within a row
- qkv_weight: bfloat16 [1024, 3, 1024], P('seq', None, 'head'), may hold values from -0.1875 to 0.1875
- out_weight: bfloat16 [1024, 1024], P('seq', 'head'), may hold values from -0.1875 to 0.1875
- cotangent: bfloat16 [4, 8, 512, 1024], P(('groups', 'dp'), 'seq', None, 'head'), parts along dimension 0, may hold values from -6 to 6
Outputs:
- layer_out: bfloat16 [4, 8, 512, 1024], P(('groups', 'dp'), 'seq', None, 'head'), parts along dimension 0
- output_weight_gradient: float32 [2048, 1024], P(('groups', 'seq'), 'head'), parts along dimension 0
There are 2 independent parts, one for each index of `groups`. A program takes and returns all parts, laid end to end along the dimension named above; an argument that names none is the same for every part. Nothing has to cross between parts.
Inputs may be any that keep to these rules, and one draw needn't show every extreme that they name: `log_decay`: never positive. `seg_lengths`: each row sums to 4096; a segment's state is reset at its first token.
All inputs are finite; a program needn't handle non-finite values.
Results may differ from a plain program's by a relative error of at most 0.0073.
Values may be sent and summed in bfloat16 or wider, within the bound.
A program may use at most 64 MiB of HBM per device.

v0:
```python
from functools import partial
import jax
import jax.numpy as jnp
from jax import lax
from jax.sharding import PartitionSpec as P


def shifted(value, axis, steps):
    count = lax.axis_size(axis)
    initial, last = (max(0, -steps), min(count, count - steps))
    return lax.ppermute(value, axis, [(source, source + steps) for source in range(initial, last)])


def block_step(carry_state, queries, key_rows, values_in, log_rates, segment, previous):
    head_scale = queries.shape[-1] ** (-0.5)
    cumulative = jnp.cumsum(log_rates, axis=-1)
    size_here = log_rates.shape[-1]
    order_idx = jnp.arange(size_here)
    allowed = (order_idx[:, None] >= order_idx[None, :]) & (segment[:, None] == segment[None, :])
    spread = cumulative[:, :, None] - cumulative[:, None, :]
    weight = jnp.where(allowed[None], jnp.exp(jnp.where(allowed[None], spread, 0.0)), 0.0)
    scores = jnp.einsum("htd,hsd->hts", queries, key_rows, preferred_element_type=jnp.float32)
    mixing = (scores * head_scale * weight).astype(jnp.bfloat16)
    inner_sum = jnp.einsum("hts,hsd->htd", mixing, values_in, preferred_element_type=jnp.float32)
    kept_mask = (segment == previous).astype(jnp.float32)
    carried = jnp.einsum(
        "htd,hde->hte", queries.astype(jnp.float32), carry_state, precision=lax.Precision.HIGHEST
    )
    result = (
        inner_sum
        + kept_mask[None, :, None] * jnp.exp(cumulative)[:, :, None] * carried * head_scale
    )
    last_seg = segment[-1]
    tail_decay = (
        jnp.exp(cumulative[:, -1:] - cumulative)
        * (segment == last_seg).astype(jnp.float32)[None, :]
    )
    decayed = (key_rows.astype(jnp.float32) * tail_decay[:, :, None]).astype(jnp.bfloat16)
    fresh = jnp.einsum("hsd,hse->hde", decayed, values_in, preferred_element_type=jnp.float32)
    through = jnp.exp(cumulative[:, -1]) * (last_seg == previous).astype(jnp.float32)
    return (through[:, None, None] * carry_state + fresh, result)


def to_blocks(array, count):
    moved = array.reshape((array.shape[0], count, array.shape[1] // count) + array.shape[2:])
    return jnp.moveaxis(moved, 1, 0)


def local_pass(queries, key_rows, values_in, log_rates, segment, before, block_size):
    heads_here, length, head_dim = queries.shape
    count = length // block_size
    seg_blocks = segment.reshape(count, block_size)
    previous = jnp.concatenate([jnp.reshape(before, (1,)), seg_blocks[:-1, -1]])

    def advance(carry_state, slab_in):
        q_blk, k_blk, v_blk, r_blk, s_blk, p_blk = slab_in
        return block_step(carry_state, q_blk, k_blk, v_blk, r_blk, s_blk, p_blk)

    start_state = jnp.zeros((heads_here, head_dim, head_dim), jnp.float32)
    final_state, block_outs = lax.scan(
        advance,
        start_state,
        (
            to_blocks(queries, count),
            to_blocks(key_rows, count),
            to_blocks(values_in, count),
            to_blocks(log_rates, count),
            seg_blocks,
            previous,
        ),
    )
    outputs = jnp.moveaxis(block_outs, 0, 1).reshape(heads_here, length, head_dim)
    return (outputs, final_state)


def local(latents, log_decay, seg_lengths, qkv_weight, out_weight, cotangent):
    strips, rate_strips = (
        lax.all_to_all(latents, "seq", split_axis=1, concat_axis=2, tiled=True),
        lax.all_to_all(log_decay, "seq", split_axis=1, concat_axis=2, tiled=True),
    )
    features = lax.all_gather(strips, "head", axis=3, tiled=True)
    proj_full, out_full = (
        lax.all_gather(qkv_weight, "seq", axis=0, tiled=True),
        lax.all_gather(out_weight, "seq", axis=0, tiled=True),
    )
    drives_here, rows_here, columns, feature_width = features.shape
    tokens_here = rows_here * columns
    heads_here = rate_strips.shape[3]
    head_dim = proj_full.shape[2] // heads_here
    block_size = min(512, tokens_here)
    split_weight = proj_full.reshape(feature_width, 3, heads_here, head_dim)
    projected = jnp.einsum(
        "bsaf,fchd->cbhsad", features, split_weight, preferred_element_type=jnp.float32
    ).astype(jnp.bfloat16)
    projected = projected.reshape(3, drives_here, heads_here, tokens_here, head_dim)
    log_rates = jnp.transpose(rate_strips.astype(jnp.float32), (0, 3, 1, 2)).reshape(
        drives_here, heads_here, tokens_here
    )
    starts = jnp.cumsum(seg_lengths, axis=1) - seg_lengths
    first_pos = lax.axis_index("seq") * tokens_here
    position = first_pos + jnp.arange(tokens_here, dtype=jnp.int32)
    segment = jnp.sum((starts[:, :, None] <= position[None, None, :]).astype(jnp.int32), axis=1) - 1
    before = jnp.sum((starts <= first_pos - 1).astype(jnp.int32), axis=1) - 1
    run_local = jax.vmap(partial(local_pass, block_size=block_size))
    local_out, own_state = run_local(
        projected[0], projected[1], projected[2], log_rates, segment, before
    )
    running = jnp.cumsum(log_rates, axis=2)
    joined_seg = (segment[:, -1] == before).astype(jnp.float32)
    self_decay = jnp.exp(running[:, :, -1]) * joined_seg[:, None]

    def relay(step_index, incoming):
        return shifted(self_decay[:, :, None, None] * incoming + own_state, "seq", 1)

    prefix = lax.fori_loop(0, lax.axis_size("seq") - 1, relay, jnp.zeros_like(own_state))
    head_scale = head_dim ** (-0.5)
    kept_mask = (segment == before[:, None]).astype(jnp.float32)
    carried = jnp.einsum(
        "bhtd,bhde->bhte", projected[0].astype(jnp.float32), prefix, precision=lax.Precision.HIGHEST
    )
    combined = (
        local_out
        + kept_mask[:, None, :, None] * jnp.exp(running)[:, :, :, None] * head_scale * carried
    )
    normed = combined * lax.rsqrt(jnp.mean(combined * combined, axis=-1, keepdims=True) + 1e-06)
    attn_rows = jnp.transpose(normed.astype(jnp.bfloat16), (0, 2, 1, 3)).reshape(
        drives_here * tokens_here, heads_here * head_dim
    )
    attn_full = lax.all_gather(attn_rows, "head", axis=1, tiled=True)
    layer_out = jnp.dot(attn_full, out_full, preferred_element_type=jnp.float32).astype(
        jnp.bfloat16
    )
    layer_out = layer_out.reshape(drives_here, rows_here, columns, out_full.shape[1])
    cot_rows = cotangent.reshape(drives_here * tokens_here, cotangent.shape[3])
    factor = float(lax.axis_size("dp") * lax.axis_size("seq") * drives_here * tokens_here) ** (-0.5)
    my_rows = lax.psum_scatter(
        lax.dot_general(
            attn_full, cot_rows, (((0,), (0,)), ((), ())), preferred_element_type=jnp.float32
        )
        * factor,
        "seq",
        scatter_dimension=0,
        tiled=True,
    )
    weight_grad = lax.psum(my_rows, "dp")
    return (layer_out, weight_grad)


def solution(mesh):
    in_specs = (
        P(("groups", "dp"), None, "seq", "head"),
        P(("groups", "dp"), None, "seq", "head"),
        P(("groups", "dp"), None),
        P("seq", None, "head"),
        P("seq", "head"),
        P(("groups", "dp"), "seq", None, "head"),
    )
    out_specs = (P(("groups", "dp"), "seq", None, "head"), P(("groups", "seq"), "head"))
    return jax.shard_map(local, mesh=mesh, in_specs=in_specs, out_specs=out_specs, check_vma=False)
```

profile of v0, /device:TPU:0, one launch (start us, length us, event | category | flops | bytes accessed | tf_op | source)
XLA Modules:
  0.0 310.2 jit_solution(2354458996665151048)
XLA Ops:
  8.0 56.2 %all_to_all.27 = bf16[1,8,128,512]{3,2,0,1:T(8,128)(2,1)S(1)} all-to-all(bf16[1,8,128,512]{3,2,0,1:T(8,128)(2,1)} %bitcast.208), channel_id=1, replica_groups=mesh['groups'=2,'seq'=4,'dp'=2,'head'=2] {'seq'}, dimensions={1} | all-to-all | bytes 2097152 | tf_op jit(solution)/shard_map/all_to_all | solution.py:78
  65.2 5.1 %all-to-all-start = ((bf16[1,8,128,4]{2,3,0,1:T(4,128)(2,1)}), bf16[1,8,128,4]{2,3,0,1:T(4,128)(2,1)S(1)}, u32[]{:S(2)}, u32[]{:S(2)}) async-start(bf16[1,8,128,4]{2,3,0,1:T(4,128)(2,1)} %bitcast.1), calls=%async_computation | async-start | bytes 16384 | tf_op jit(solution)/shard_map/all_to_all | solution.py:79
  78.1 13.0 %all-gather.5.cloned.1.call-done = bf16[1024,3,512]{2,0,1:T(8,128)(2,1)} async-done(((bf16[256,3,512]{2,0,1:T(8,128)(2,1)}), bf16[1024,3,512]{2,0,1:T(8,128)(2,1)}) %all-gather.5.cloned.1.call-update) | async-done | bytes 3145744 | tf_op jit(solution)/shard_map/all_gather | solution.py:83
  91.1 4.7 %copy.65 = bf16[1024,3,512]{0,2,1:T(8,128)(2,1)} copy(bf16[1024,3,512]{2,0,1:T(8,128)(2,1)} %all-gather.5.cloned.1.call-done) | data formatting | bytes 6291456 | tf_op jit(solution)/shard_map/all_gather | solution.py:83
  95.8 7.3 %all-gather.7.cloned.1.call-done = bf16[1,2,512,1024]{3,2,1,0:T(8,128)(2,1)} async-done(((bf16[1,2,512,512]{3,2,1,0:T(8,128)(2,1)}), bf16[1,2,512,1024]{3,2,1,0:T(8,128)(2,1)}) %all-gather.7.cloned.1.call-update) | async-done | bytes 2097168 | tf_op jit(solution)/shard_map/all_gather | solution.py:81
  103.1 6.1 %convert_bitcast_fusion = bf16[3,1,4,2,512,128]{4,5,3,2,0,1:T(8,128)(2,1)S(1)} fusion(bf16[1024,3,4,128,1]{0,3,4,2,1:T(8,128)(2,1)} %bitcast.204, bf16[1,2,512,1024]{3,2,1,0:T(8,128)(2,1)} %all-gather.7.cloned.1.call-done), kind=kOutput, calls=%fused_computation.48 | convolution fusion | flops 3222798336 | bytes 8388608 | tf_op jit(solution)/shard_map/bsaf,fchd->cbhsad/dot_general | solution.py:92
  111.4 29.2 %while.24 = (s32[]{:T(128)}, f32[1,4,128,128]{3,2,1,0:T(8,128)S(1)}, f32[2,1,4,512,128]{4,3,2,1,0:T(8,128)}, f32[2,1,4,512]{3,2,1,0:T(4,128)S(1)}, s32[2,1,512]{...) while((s32[]{:T(128)}, ...), condition=%wide.region_6.7_spmd.clone, body=%wide.region_3.6_spmd.clone.sunk | while | flops 1015816256 | bytes 14092170 | solution.py:60
  114.6 3.5 %fusion.69 = f32[4,512,128]{2,1,0:T(8,128)S(1)} fusion(f32[4,512]{1,0:T(4,128)S(1)} %get-tuple-element.263, pred[512,512]{1,0:T(8,128)(4,1)S(1)} %fusion.68, bf16[2,1,4,512,128]{3,4,0,2,1:T(8,128)(2,1)} %get-tuple-element.299, s32[]{:T(128)} %get-tuple-element.279, bf16[2,1,4,512,128]{3,4,0,2,1:T(8,128)(2,1)} %get-tuple-element.298, ...), kind=kOutput, calls=%fused_computation.2.clone.1 | convolution fusion | flops 543162368 | bytes 2901504 | tf_op jit(solution)/shard_map/vmap()/while/body/eval_jaxpr/hts,hsd->htd/dot_general | solution.py:24
  129.2 3.5 %fusion.69 = f32[4,512,128]{2,1,0:T(8,128)S(1)} fusion(f32[4,512]{1,0:T(4,128)S(1)} %get-tuple-element.263, pred[512,512]{1,0:T(8,128)(4,1)S(1)} %fusion.68, bf16[2,1,4,512,128]{3,4,0,2,1:T(8,128)(2,1)} %get-tuple-element.299, s32[]{:T(128)} %get-tuple-element.279, bf16[2,1,4,512,128]{3,4,0,2,1:T(8,128)(2,1)} %get-tuple-element.298, ...), kind=kOutput, calls=%fused_computation.2.clone.1 | convolution fusion | flops 543162368 | bytes 2901504 | tf_op jit(solution)/shard_map/vmap()/while/body/eval_jaxpr/hts,hsd->htd/dot_general | solution.py:24
  140.5 2.9 copy.72
  147.9 28.2 %while.23 = (s32[]{:T(128)}, f32[1,4,128,128]{3,2,1,0:T(8,128)S(1)}, f32[1,4]{1,0:T(1,128)S(1)}, f32[1,4,128,128]{3,2,1,0:T(8,128)S(1)}, s32[]{:T(128)}) while((s32[]{:T(128)}, f32[1,4,128,128]{3,2,1,0:T(8,128)S(1)}, f32[1,4]{1,0:T(1,128)S(1)}, f32[1,4,128,128]{3,2,1,0:T(8,128)S(1)}, s32[]{:T(128)}) %tuple.57), condition=%wide.region_10.11_spmd, body=%wide.region_9.10_spmd.sunk | while | flops 131074 | bytes 1835125 | solution.py:115
  148.0 3.7 %collective-permute-start = (f32[1,4,128,128]{3,2,1,0:T(8,128)S(1)}, f32[1,4,128,128]{3,2,1,0:T(8,128)S(1)}, u32[]{:S(2)}, u32[]{:S(2)}) collective-permute-start(f32[1,4,128,128]{3,2,1,0:T(8,128)S(1)} %multiply_add_fusion.3), channel_id=1, source_target_pairs={{0,4},{4,8},{8,12},{1,5},{5,9},{9,13},{2,6},{6,10},{10,14},{3,7},{... | collective-permute-start | bytes 786440 | tf_op jit(solution)/shard_map/while/body/eval_jaxpr/ppermute | solution.py:11
  151.7 6.0 %collective-permute-done = f32[1,4,128,128]{3,2,1,0:T(8,128)S(1)} collective-permute-done((f32[1,4,128,128]{3,2,1,0:T(8,128)S(1)}, f32[1,4,128,128]{3,2,1,0:T(8,128)S(1)}, u32[]{:S(2)}, u32[]{:S(2)}) %collective-permute-start) | collective-permute-done | bytes 262176 | tf_op jit(solution)/shard_map/while/body/eval_jaxpr/ppermute | solution.py:11
  157.8 4.4 %collective-permute-start = (f32[1,4,128,128]{3,2,1,0:T(8,128)S(1)}, f32[1,4,128,128]{3,2,1,0:T(8,128)S(1)}, u32[]{:S(2)}, u32[]{:S(2)}) collective-permute-start(f32[1,4,128,128]{3,2,1,0:T(8,128)S(1)} %multiply_add_fusion.3), channel_id=1, source_target_pairs={{0,4},{4,8},{8,12},{1,5},{5,9},{9,13},{2,6},{6,10},{10,14},{3,7},{... | collective-permute-start | bytes 786440 | tf_op jit(solution)/shard_map/while/body/eval_jaxpr/ppermute | solution.py:11
  162.2 5.2 %collective-permute-done = f32[1,4,128,128]{3,2,1,0:T(8,128)S(1)} collective-permute-done((f32[1,4,128,128]{3,2,1,0:T(8,128)S(1)}, f32[1,4,128,128]{3,2,1,0:T(8,128)S(1)}, u32[]{:S(2)}, u32[]{:S(2)}) %collective-permute-start) | collective-permute-done | bytes 262176 | tf_op jit(solution)/shard_map/while/body/eval_jaxpr/ppermute | solution.py:11
  167.5 4.4 %collective-permute-start = (f32[1,4,128,128]{3,2,1,0:T(8,128)S(1)}, f32[1,4,128,128]{3,2,1,0:T(8,128)S(1)}, u32[]{:S(2)}, u32[]{:S(2)}) collective-permute-start(f32[1,4,128,128]{3,2,1,0:T(8,128)S(1)} %multiply_add_fusion.3), channel_id=1, source_target_pairs={{0,4},{4,8},{8,12},{1,5},{5,9},{9,13},{2,6},{6,10},{10,14},{3,7},{... | collective-permute-start | bytes 786440 | tf_op jit(solution)/shard_map/while/body/eval_jaxpr/ppermute | solution.py:11
  171.9 4.3 %collective-permute-done = f32[1,4,128,128]{3,2,1,0:T(8,128)S(1)} collective-permute-done((f32[1,4,128,128]{3,2,1,0:T(8,128)S(1)}, f32[1,4,128,128]{3,2,1,0:T(8,128)S(1)}, u32[]{:S(2)}, u32[]{:S(2)}) %collective-permute-start) | collective-permute-done | bytes 262176 | tf_op jit(solution)/shard_map/while/body/eval_jaxpr/ppermute | solution.py:11
  176.2 2.9 multiply_reduce_fusion
  180.4 12.6 %all-gather.9.cloned.1.call-done = bf16[1024,1024]{0,1:T(8,128)(2,1)} async-done(((bf16[1024,512]{0,1:T(8,128)(2,1)}), bf16[1024,1024]{0,1:T(8,128)(2,1)}) %all-gather.9.cloned.1.call-update) | async-done | bytes 2097168 | tf_op jit(solution)/shard_map/all_gather | solution.py:129
  193.0 4.1 %convolution_multiply_fusion.1 = f32[1024,512]{1,0:T(8,128)} fusion(bf16[1024,1024]{0,1:T(8,128)(2,1)} %all-gather.9.cloned.1.call-done, bf16[1024,512]{1,0:T(8,128)(2,1)S(1)} %bitcast.196), kind=kOutput, calls=%fused_computation.53 | convolution fusion | flops 1074266112 | bytes 5242880 | tf_op jit(solution)/shard_map/dot_general | solution.py:137
  197.8 44.5 %reduce-scatter.2.cloned.1.call-done = f32[256,512]{1,0:T(8,128)} async-done(((f32[1024,512]{1,0:T(8,128)}), f32[256,512]{1,0:T(8,128)}) %reduce-scatter.2.cloned.1.call-update) | async-done | bytes 524304 | tf_op jit(solution)/shard_map/reduce_scatter | solution.py:136
  242.4 28.8 %all-gather.11.cloned.1.call-done = bf16[1024,512]{1,0:T(8,128)(2,1)} async-done(((bf16[256,512]{1,0:T(8,128)(2,1)}), bf16[1024,512]{1,0:T(8,128)(2,1)}) %all-gather.11.cloned.1.call-update) | async-done | bytes 1048592 | tf_op jit(solution)/shard_map/all_gather | solution.py:84
  271.1 3.5 %convolution_convert_fusion = bf16[1024,512]{1,0:T(8,128)(2,1)} fusion(bf16[1024,1024]{0,1:T(8,128)(2,1)S(1)} %copy-done.3, bf16[1024,512]{1,0:T(8,128)(2,1)} %all-gather.11.cloned.1.call-done), kind=kOutput, calls=%fused_computation.54 | convolution fusion | flops 1074266112 | bytes 4194304 | tf_op jit(solution)/shard_map/dot_general | solution.py:130
  274.6 26.9 %all-reduce.2.cloned.1.call-done = f32[256,512]{1,0:T(8,128)} async-done(((f32[256,512]{1,0:T(8,128)}), f32[256,512]{1,0:T(8,128)}) %all-reduce.2.cloned.1.call-update) | async-done | bytes 524304 | tf_op jit(solution)/shard_map/psum | solution.py:145
  (109 shorter events, 38.6 us)
Async XLA Ops:
  7.2 185.8 %copy-start = (bf16[1,2,512,512]{3,2,1,0:T(8,128)(2,1)S(1)}, bf16[1,2,512,512]{3,2,1,0:T(8,128)(2,1)}, u32[]{:S(2)}) copy-start(bf16[1,2,512,512]{3,2,1,0:T(8,128)(2,1)} %param.15) | copy-start | bytes 3145732
  7.2 83.9 %all-gather.5.cloned.1.call-start = ((), (), s32[]{:S(2)}) async-start(), calls=%async_computation.3 | async-start | bytes 3932160 | tf_op jit(solution)/shard_map/all_gather | solution.py:83
  7.9 95.2 %all-gather.7.cloned.1.call-start = ((), (), s32[]{:S(2)}) async-start(), calls=%async_computation.4 | async-start | bytes 3145728 | tf_op jit(solution)/shard_map/all_gather | solution.py:81
  64.1 6.2 %copy-start.2 = (s32[1,4]{1,0:T(1,128)S(1)}, s32[1,4]{1,0:T(1,128)}, u32[]{:S(2)}) copy-start(s32[1,4]{1,0:T(1,128)} %param.12) | copy-start | bytes 52
  65.2 10.7 %all-to-all-start = ((bf16[1,8,128,4]{2,3,0,1:T(4,128)(2,1)}), bf16[1,8,128,4]{2,3,0,1:T(4,128)(2,1)S(1)}, u32[]{:S(2)}, u32[]{:S(2)}) async-start(bf16[1,8,128,4]{2,3,0,1:T(4,128)(2,1)} %bitcast.1), calls=%async_computation | async-start | bytes 16384 | tf_op jit(solution)/shard_map/all_to_all | solution.py:79
  70.4 122.6 %all-gather.9.cloned.1.call-start = ((), (), s32[]{:S(2)}) async-start(), calls=%async_computation.5 | async-start | bytes 3145728 | tf_op jit(solution)/shard_map/all_gather | solution.py:129
  120.9 4.1 %copy-start.1 = (bf16[2,1,4,512,128]{3,4,0,2,1:T(8,128)(2,1)S(1)}, bf16[2,1,4,512,128]{3,4,0,2,1:T(8,128)(2,1)}, u32[]{:S(2)}) copy-start(bf16[2,1,4,512,128]{3,4,0,2,1:T(8,128)(2,1)} %get-tuple-element.298) | copy-start | bytes 3145732 | tf_op jit(solution)/shard_map/vmap()/while
  135.5 4.1 %copy-start.1 = (bf16[2,1,4,512,128]{3,4,0,2,1:T(8,128)(2,1)S(1)}, bf16[2,1,4,512,128]{3,4,0,2,1:T(8,128)(2,1)}, u32[]{:S(2)}) copy-start(bf16[2,1,4,512,128]{3,4,0,2,1:T(8,128)(2,1)} %get-tuple-element.298) | copy-start | bytes 3145732 | tf_op jit(solution)/shard_map/vmap()/while
  148.0 9.7 %collective-permute-start = (f32[1,4,128,128]{3,2,1,0:T(8,128)S(1)}, f32[1,4,128,128]{3,2,1,0:T(8,128)S(1)}, u32[]{:S(2)}, u32[]{:S(2)}) collective-permute-start(f32[1,4,128,128]{3,2,1,0:T(8,128)S(1)} %multiply_add_fusion.3), channel_id=1, source_target_pairs={{0,4},{4,8},{8,12},{1,5},{5,9},{9,13},{2,6},{6,10},{10,14},{3,7},{... | collective-permute-start | bytes 786440 | tf_op jit(solution)/shard_map/while/body/eval_jaxpr/ppermute | solution.py:11
  157.8 9.6 %collective-permute-start = (f32[1,4,128,128]{3,2,1,0:T(8,128)S(1)}, f32[1,4,128,128]{3,2,1,0:T(8,128)S(1)}, u32[]{:S(2)}, u32[]{:S(2)}) collective-permute-start(f32[1,4,128,128]{3,2,1,0:T(8,128)S(1)} %multiply_add_fusion.3), channel_id=1, source_target_pairs={{0,4},{4,8},{8,12},{1,5},{5,9},{9,13},{2,6},{6,10},{10,14},{3,7},{... | collective-permute-start | bytes 786440 | tf_op jit(solution)/shard_map/while/body/eval_jaxpr/ppermute | solution.py:11
  167.5 8.7 %collective-permute-start = (f32[1,4,128,128]{3,2,1,0:T(8,128)S(1)}, f32[1,4,128,128]{3,2,1,0:T(8,128)S(1)}, u32[]{:S(2)}, u32[]{:S(2)}) collective-permute-start(f32[1,4,128,128]{3,2,1,0:T(8,128)S(1)} %multiply_add_fusion.3), channel_id=1, source_target_pairs={{0,4},{4,8},{8,12},{1,5},{5,9},{9,13},{2,6},{6,10},{10,14},{3,7},{... | collective-permute-start | bytes 786440 | tf_op jit(solution)/shard_map/while/body/eval_jaxpr/ppermute | solution.py:11
  180.3 62.0 %reduce-scatter.2.cloned.1.call-start = ((), (), s32[]{:S(2)}) async-start(), calls=%async_computation.7 | async-start | bytes 2621440 | tf_op jit(solution)/shard_map/reduce_scatter | solution.py:136
  197.1 74.0 %copy-start.3 = (bf16[1024,1024]{0,1:T(8,128)(2,1)S(1)}, bf16[1024,1024]{0,1:T(8,128)(2,1)}, u32[]{:S(2)}) copy-start(bf16[1024,1024]{0,1:T(8,128)(2,1)} %all-gather.9.cloned.1.call-done) | copy-start | bytes 6291460
  197.1 74.0 %all-gather.11.cloned.1.call-start = ((), (), s32[]{:S(2)}) async-start(), calls=%async_computation.6 | async-start | bytes 1310720 | tf_op jit(solution)/shard_map/all_gather | solution.py:84
  197.7 103.8 %all-reduce.2.cloned.1.call-start = ((), (), s32[]{:S(2)}) async-start(), calls=%async_computation.8 | async-start | bytes 1048576 | tf_op jit(solution)/shard_map/psum | solution.py:145
Sparse Core Ops, SparseCore 0:
  9.6 81.4 all-gather.4
  93.2 9.8 all-gather.6
  180.5 12.4 all-gather.8
  197.3 45.0 reduce-scatter.1
  243.8 27.2 all-gather.10
  273.4 28.0 all-reduce.1
where the time goes:
time: 311 us; the launch traced here: 310 us
  waiting for transfers between devices  151 us (49%)
  blocking collectives  56.2 us (18%)
  matrix products  31.1 us (10%)
  local copies, waits for them, and re-layouts  25.4 us (8%)
  starting transfers between devices  17.8 us (6%)
  between operations  15.5 us (5%)
  other arithmetic  10.4 us (3%)
    all_to_all x1, blocking collectives, local(): lax.all_to_all(latents, 'seq', split_axis=1, concat_axis=2, tiled=True)  56.2 us
    reduce_scatter x1, waiting for transfers between devices, local(): lax.psum_scatter(lax.dot_general(attn_full, cot_rows, (((0,), (0,)), ((),...  44.5 us
    all_gather x1, waiting for transfers between devices, local(): lax.all_gather(out_weight, 'seq', axis=0, tiled=True)  28.8 us
    psum x1, waiting for transfers between devices, local(): weight_grad = lax.psum(my_rows, 'dp')  26.9 us
    ppermute x3, waiting for transfers between devices, shifted(): lax.ppermute(value, axis, [(source, source + steps) for source in range(i...  15.4 us
    all_gather x1, waiting for transfers between devices, local(): lax.all_gather(qkv_weight, 'seq', axis=0, tiled=True)  13 us
    all_gather x1, waiting for transfers between devices, local(): attn_full = lax.all_gather(attn_rows, 'head', axis=1, tiled=True)  12.6 us
    ppermute x3, starting transfers between devices, shifted(): lax.ppermute(value, axis, [(source, source + steps) for source in range(i...  12.5 us
  transfers between devices with their start and end apart: 10, of which 10 were waited for; matrix products, arithmetic and copies ran while one was open for 5% of the time, Pallas kernels for 0%

commit v1 on v0

--- a/solution.py
+++ b/solution.py
@@ -3,6 +3,19 @@
 import jax.numpy as jnp
 from jax import lax
 from jax.sharding import PartitionSpec as P
+
+
+def ring_gather(value, axis, dim):
+    ways = lax.axis_size(axis)
+    up = [(d, (d + 1) % ways) for d in range(ways)]
+    down = [(d, (d - 1) % ways) for d in range(ways)]
+    earlier, later = ([value], [value])
+    for _ in range(ways // 2):
+        earlier.append(lax.ppermute(earlier[-1], axis, up))
+    for _ in range((ways - 1) // 2):
+        later.append(lax.ppermute(later[-1], axis, down))
+    line = jnp.concatenate([*earlier[::-1], *later[1:]], axis=dim)
+    return jnp.roll(line, (lax.axis_index(axis) - ways // 2) * value.shape[dim], axis=dim)
 
 
 def shifted(value, axis, steps):
@@ -80,7 +93,7 @@
     )
     features = lax.all_gather(strips, "head", axis=3, tiled=True)
     proj_full, out_full = (
-        lax.all_gather(qkv_weight, "seq", axis=0, tiled=True),
+        ring_gather(qkv_weight, "seq", 0),
         lax.all_gather(out_weight, "seq", axis=0, tiled=True),
     )
     drives_here, rows_here, columns, feature_width = features.shape

time: 311 us -> 310 us (level)
  blocking collectives: 56.2 us -> 0 us
  waiting for transfers between devices: 151 us -> 186 us
  local copies, waits for them, and re-layouts: 25.4 us -> 34.8 us
  starting transfers between devices: 17.8 us -> 24.4 us
    all_to_all x1 -> x0, blocking collectives: 56.2 us -> none  [local(): lax.all_to_all(latents, 'seq', split_axis=1, concat_axis=2, tiled=True)]
    all_to_all x0 -> x1, waiting for transfers between devices: none -> 36.3 us  [local(): lax.all_to_all(latents, 'seq', split_axis=1, concat_axis=2, tiled=True)]
    ppermute x0 -> x3, waiting for transfers between devices: none -> 16.6 us  [the longest x2 16.6 us: ring_gather(): earlier.append(lax.ppermute(earlier[-1], axis, up))]
    all_gather x1 -> x0, waiting for transfers between devices: 13 us -> none  [local(): lax.all_gather(qkv_weight, 'seq', axis=0, tiled=True)]
    all_to_all x1, waiting for transfers between devices: 1.38 us -> 9.55 us  [local(): lax.all_to_all(log_decay, 'seq', split_axis=1, concat_axis=2, tiled=True)]
    all_gather x1, waiting for transfers between devices: 7.31 us -> 0.01 us  [local(): features = lax.all_gather(strips, 'head', axis=3, tiled=True)]
    dynamic_slice x0 -> x2, local copies, waits for them, and re-layouts: none -> 6.59 us  [ring_gather(): jnp.roll(line, (lax.axis_index(axis) - ways // 2) * value.shape[dim], axi...]
    all_to_all x0 -> x1, starting transfers between devices: none -> 6.46 us  [local(): lax.all_to_all(latents, 'seq', split_axis=1, concat_axis=2, tiled=True)]
  transfers between devices with their start and end apart: 10 -> 13, of which waited for: 10 -> 10; matrix products, arithmetic and copies ran while one was open for 5% -> 8% of each run, Pallas kernels for 0% -> 0%
where the time goes in v1:
time: 310 us; the launch traced here: 308 us
  waiting for transfers between devices  186 us (60%)
  local copies, waits for them, and re-layouts  34.8 us (11%)
  matrix products  33 us (11%)
  starting transfers between devices  24.4 us (8%)
  between operations  15.3 us (5%)
  other arithmetic  12.4 us (4%)
    reduce_scatter x1, waiting for transfers between devices, local(): lax.psum_scatter(lax.dot_general(attn_full, cot_rows, (((0,), (0,)), ((),...  44.6 us
    all_to_all x1, waiting for transfers between devices, local(): lax.all_to_all(latents, 'seq', split_axis=1, concat_axis=2, tiled=True)  36.3 us
    all_gather x1, waiting for transfers between devices, local(): lax.all_gather(out_weight, 'seq', axis=0, tiled=True)  28.7 us
    psum x1, waiting for transfers between devices, local(): weight_grad = lax.psum(my_rows, 'dp')  26.9 us
    ppermute x2, waiting for transfers between devices, ring_gather(): earlier.append(lax.ppermute(earlier[-1], axis, up))  16.6 us
    ppermute x3, waiting for transfers between devices, shifted(): lax.ppermute(value, axis, [(source, source + steps) for source in range(i...  11.6 us
    all_gather x1, waiting for transfers between devices, local(): attn_full = lax.all_gather(attn_rows, 'head', axis=1, tiled=True)  11 us
    ppermute x3, starting transfers between devices, shifted(): lax.ppermute(value, axis, [(source, source + steps) for source in range(i...  10.1 us
  transfers between devices with their start and end apart: 13, of which 10 were waited for; matrix products, arithmetic and copies ran while one was open for 8% of the time, Pallas kernels for 0%

profile of v1, /device:TPU:0, one launch (start us, length us, event | category | flops | bytes accessed | tf_op | source)
XLA Modules:
  0.0 308.4 jit_solution(11740517687152217870)
XLA Ops:
  7.2 6.5 %all-to-all-start.1 = ((bf16[1,8,128,512]{3,2,0,1:T(8,128)(2,1)}), bf16[1,8,128,512]{3,2,0,1:T(8,128)(2,1)S(1)}, u32[]{:S(2)}, u32[]{:S(2)}) async-start(bf16[1,8,128,512]{3,2,0,1:T(8,128)(2,1)} %bitcast.208), calls=%async_computation.1 | async-start | bytes 2097152 | tf_op jit(solution)/shard_map/all_to_all | solution.py:91
  21.0 36.3 %all-to-all-done.1 = bf16[1,8,128,512]{3,2,0,1:T(8,128)(2,1)S(1)} async-done(((bf16[1,8,128,512]{3,2,0,1:T(8,128)(2,1)}), bf16[1,8,128,512]{3,2,0,1:T(8,128)(2,1)S(1)}, u32[]{:S(2)}, u32[]{:S(2)}) %all-to-all-start.1) | async-done | bytes 1048608 | tf_op jit(solution)/shard_map/all_to_all | solution.py:91
  57.3 3.2 %all-to-all-start = ((bf16[1,8,128,4]{2,3,0,1:T(4,128)(2,1)}), bf16[1,8,128,4]{2,3,0,1:T(4,128)(2,1)S(1)}, u32[]{:S(2)}, u32[]{:S(2)}) async-start(bf16[1,8,128,4]{2,3,0,1:T(4,128)(2,1)} %bitcast.221), calls=%async_computation | async-start | bytes 16384 | tf_op jit(solution)/shard_map/all_to_all | solution.py:92
  63.7 9.5 %all-to-all-done = bf16[1,8,128,4]{2,3,0,1:T(4,128)(2,1)S(1)} async-done(((bf16[1,8,128,4]{2,3,0,1:T(4,128)(2,1)}), bf16[1,8,128,4]{2,3,0,1:T(4,128)(2,1)S(1)}, u32[]{:S(2)}, u32[]{:S(2)}) %all-to-all-start) | async-done | bytes 8224 | tf_op jit(solution)/shard_map/all_to_all | solution.py:92
  79.3 16.6 %collective-permute-done.2 = bf16[256,3,512]{2,0,1:T(8,128)(2,1)} collective-permute-done((bf16[256,3,512]{2,0,1:T(8,128)(2,1)}, bf16[256,3,512]{2,0,1:T(8,128)(2,1)}, u32[]{:S(2)}, u32[]{:S(2)}) %collective-permute-start.2) | collective-permute-done | bytes 786464 | tf_op jit(solution)/shard_map/ppermute | solution.py:14
  102.8 4.7 %copy.65 = bf16[1024,3,512]{0,2,1:T(8,128)(2,1)} copy(bf16[1024,3,512]{2,0,1:T(8,128)(2,1)} %constant_dynamic-slice_fusion.6) | data formatting | bytes 6291456 | tf_op jit(solution)/shard_map/jit(_roll_dynamic)/dynamic_slice | solution.py:18
  107.5 6.0 %convert_bitcast_fusion = bf16[3,1,4,2,512,128]{4,5,3,2,0,1:T(8,128)(2,1)S(1)} fusion(bf16[1024,3,4,128,1]{0,3,4,2,1:T(8,128)(2,1)} %bitcast.204, bf16[1,2,512,1024]{3,2,1,0:T(8,128)(2,1)} %all-gather.4.cloned.1.call-done), kind=kOutput, calls=%fused_computation.48 | convolution fusion | flops 3222798336 | bytes 8388608 | tf_op jit(solution)/shard_map/bsaf,fchd->cbhsad/dot_general | solution.py:105
  115.7 31.0 %while.24 = (s32[]{:T(128)}, f32[1,4,128,128]{3,2,1,0:T(8,128)S(1)}, f32[2,1,4,512,128]{4,3,2,1,0:T(8,128)}, f32[2,1,4,512]{3,2,1,0:T(4,128)S(1)}, s32[2,1,512]{...) while((s32[]{:T(128)}, ...), condition=%wide.region_6.7_spmd.clone, body=%wide.region_3.6_spmd.clone.sunk | while | flops 1015816256 | bytes 9897850 | solution.py:73
  119.1 3.5 %fusion.69 = f32[4,512,128]{2,1,0:T(8,128)S(1)} fusion(f32[4,512]{1,0:T(4,128)S(1)} %get-tuple-element.263, pred[512,512]{1,0:T(8,128)(4,1)S(1)} %fusion.68, bf16[2,1,4,512,128]{3,4,0,2,1:T(8,128)(2,1)} %get-tuple-element.299, s32[]{:T(128)} %get-tuple-element.279, bf16[2,1,4,512,128]{3,4,0,2,1:T(8,128)(2,1)} %get-tuple-element.298, ...), kind=kOutput, calls=%fused_computation.2.clone.1 | convolution fusion | flops 543162368 | bytes 2901504 | tf_op jit(solution)/shard_map/vmap()/while/body/eval_jaxpr/hts,hsd->htd/dot_general | solution.py:37
  134.6 3.5 %fusion.69 = f32[4,512,128]{2,1,0:T(8,128)S(1)} fusion(f32[4,512]{1,0:T(4,128)S(1)} %get-tuple-element.263, pred[512,512]{1,0:T(8,128)(4,1)S(1)} %fusion.68, bf16[2,1,4,512,128]{3,4,0,2,1:T(8,128)(2,1)} %get-tuple-element.299, s32[]{:T(128)} %get-tuple-element.279, bf16[2,1,4,512,128]{3,4,0,2,1:T(8,128)(2,1)} %get-tuple-element.298, ...), kind=kOutput, calls=%fused_computation.2.clone.1 | convolution fusion | flops 543162368 | bytes 2901504 | tf_op jit(solution)/shard_map/vmap()/while/body/eval_jaxpr/hts,hsd->htd/dot_general | solution.py:37
  146.8 2.9 copy.72
  154.2 22.0 %while.23 = (s32[]{:T(128)}, f32[1,4,128,128]{3,2,1,0:T(8,128)S(1)}, f32[1,4]{1,0:T(1,128)S(1)}, f32[1,4,128,128]{3,2,1,0:T(8,128)S(1)}, s32[]{:T(128)}) while((s32[]{:T(128)}, f32[1,4,128,128]{3,2,1,0:T(8,128)S(1)}, f32[1,4]{1,0:T(1,128)S(1)}, f32[1,4,128,128]{3,2,1,0:T(8,128)S(1)}, s32[]{:T(128)}) %tuple.57), condition=%wide.region_10.11_spmd, body=%wide.region_9.10_spmd.sunk | while | flops 131074 | bytes 1835125 | solution.py:128
  155.6 3.9 %collective-permute-done = f32[1,4,128,128]{3,2,1,0:T(8,128)S(1)} collective-permute-done((f32[1,4,128,128]{3,2,1,0:T(8,128)S(1)}, f32[1,4,128,128]{3,2,1,0:T(8,128)S(1)}, u32[]{:S(2)}, u32[]{:S(2)}) %collective-permute-start) | collective-permute-done | bytes 262176 | tf_op jit(solution)/shard_map/while/body/eval_jaxpr/ppermute | solution.py:24
  159.5 4.4 %collective-permute-start = (f32[1,4,128,128]{3,2,1,0:T(8,128)S(1)}, f32[1,4,128,128]{3,2,1,0:T(8,128)S(1)}, u32[]{:S(2)}, u32[]{:S(2)}) collective-permute-start(f32[1,4,128,128]{3,2,1,0:T(8,128)S(1)} %multiply_add_fusion.3), channel_id=1, source_target_pairs={{0,4},{4,8},{8,12},{1,5},{5,9},{9,13},{2,6},{6,10},{10,14},{3,7},{... | collective-permute-start | bytes 786440 | tf_op jit(solution)/shard_map/while/body/eval_jaxpr/ppermute | solution.py:24
  164.0 3.9 %collective-permute-done = f32[1,4,128,128]{3,2,1,0:T(8,128)S(1)} collective-permute-done((f32[1,4,128,128]{3,2,1,0:T(8,128)S(1)}, f32[1,4,128,128]{3,2,1,0:T(8,128)S(1)}, u32[]{:S(2)}, u32[]{:S(2)}) %collective-permute-start) | collective-permute-done | bytes 262176 | tf_op jit(solution)/shard_map/while/body/eval_jaxpr/ppermute | solution.py:24
  167.9 4.4 %collective-permute-start = (f32[1,4,128,128]{3,2,1,0:T(8,128)S(1)}, f32[1,4,128,128]{3,2,1,0:T(8,128)S(1)}, u32[]{:S(2)}, u32[]{:S(2)}) collective-permute-start(f32[1,4,128,128]{3,2,1,0:T(8,128)S(1)} %multiply_add_fusion.3), channel_id=1, source_target_pairs={{0,4},{4,8},{8,12},{1,5},{5,9},{9,13},{2,6},{6,10},{10,14},{3,7},{... | collective-permute-start | bytes 786440 | tf_op jit(solution)/shard_map/while/body/eval_jaxpr/ppermute | solution.py:24
  172.3 3.9 %collective-permute-done = f32[1,4,128,128]{3,2,1,0:T(8,128)S(1)} collective-permute-done((f32[1,4,128,128]{3,2,1,0:T(8,128)S(1)}, f32[1,4,128,128]{3,2,1,0:T(8,128)S(1)}, u32[]{:S(2)}, u32[]{:S(2)}) %collective-permute-start) | collective-permute-done | bytes 262176 | tf_op jit(solution)/shard_map/while/body/eval_jaxpr/ppermute | solution.py:24
  176.2 2.9 multiply_reduce_fusion
  180.4 11.0 %all-gather.6.cloned.1.call-done = bf16[1024,1024]{0,1:T(8,128)(2,1)} async-done(((bf16[1024,512]{0,1:T(8,128)(2,1)}), bf16[1024,1024]{0,1:T(8,128)(2,1)}) %all-gather.6.cloned.1.call-update) | async-done | bytes 2097168 | tf_op jit(solution)/shard_map/all_gather | solution.py:142
  191.3 4.3 %convolution_multiply_fusion.1 = f32[1024,512]{1,0:T(8,128)} fusion(bf16[1024,1024]{0,1:T(8,128)(2,1)} %all-gather.6.cloned.1.call-done, bf16[1024,512]{1,0:T(8,128)(2,1)S(1)} %bitcast.196), kind=kOutput, calls=%fused_computation.53 | convolution fusion | flops 1074266112 | bytes 5242880 | tf_op jit(solution)/shard_map/dot_general | solution.py:150
  196.3 44.6 %reduce-scatter.2.cloned.1.call-done = f32[256,512]{1,0:T(8,128)} async-done(((f32[1024,512]{1,0:T(8,128)}), f32[256,512]{1,0:T(8,128)}) %reduce-scatter.2.cloned.1.call-update) | async-done | bytes 524304 | tf_op jit(solution)/shard_map/reduce_scatter | solution.py:149
  240.9 28.7 %all-gather.8.cloned.1.call-done = bf16[1024,512]{1,0:T(8,128)(2,1)} async-done(((bf16[256,512]{1,0:T(8,128)(2,1)}), bf16[1024,512]{1,0:T(8,128)(2,1)}) %all-gather.8.cloned.1.call-update) | async-done | bytes 1048592 | tf_op jit(solution)/shard_map/all_gather | solution.py:97
  269.6 3.5 %convolution_convert_fusion = bf16[1024,512]{1,0:T(8,128)(2,1)} fusion(bf16[1024,1024]{0,1:T(8,128)(2,1)S(1)} %copy-done.2, bf16[1024,512]{1,0:T(8,128)(2,1)} %all-gather.8.cloned.1.call-done), kind=kOutput, calls=%fused_computation.54 | convolution fusion | flops 1074266112 | bytes 4194304 | tf_op jit(solution)/shard_map/dot_general | solution.py:143
  273.1 26.9 %all-reduce.2.cloned.1.call-done = f32[256,512]{1,0:T(8,128)} async-done(((f32[256,512]{1,0:T(8,128)}), f32[256,512]{1,0:T(8,128)}) %all-reduce.2.cloned.1.call-update) | async-done | bytes 524304 | tf_op jit(solution)/shard_map/psum | solution.py:158
  (118 shorter events, 55.5 us)
Async XLA Ops:
  7.2 184.2 %copy-start = (bf16[1,2,512,512]{3,2,1,0:T(8,128)(2,1)S(1)}, bf16[1,2,512,512]{3,2,1,0:T(8,128)(2,1)}, u32[]{:S(2)}) copy-start(bf16[1,2,512,512]{3,2,1,0:T(8,128)(2,1)} %param.15) | copy-start | bytes 3145732
  7.2 50.1 %all-to-all-start.1 = ((bf16[1,8,128,512]{3,2,0,1:T(8,128)(2,1)}), bf16[1,8,128,512]{3,2,0,1:T(8,128)(2,1)S(1)}, u32[]{:S(2)}, u32[]{:S(2)}) async-start(bf16[1,8,128,512]{3,2,0,1:T(8,128)(2,1)} %bitcast.208), calls=%async_computation.1 | async-start | bytes 2097152 | tf_op jit(solution)/shard_map/all_to_all | solution.py:91
  13.6 61.9 %collective-permute-start.1 = (bf16[256,3,512]{2,0,1:T(8,128)(2,1)}, bf16[256,3,512]{2,0,1:T(8,128)(2,1)}, u32[]{:S(2)}, u32[]{:S(2)}) collective-permute-start(bf16[256,3,512]{2,0,1:T(8,128)(2,1)} %param.13), channel_id=1, source_target_pairs={{0,4},{4,8},{8,12},{12,0},{1,5},{5,9},{9,13},{13,1},{2,6},{6,10},{... | collective-permute-start | bytes 2359304 | tf_op jit(solution)/shard_map/ppermute | solution.py:14
  15.7 82.7 %collective-permute-start.3 = (bf16[256,3,512]{2,0,1:T(8,128)(2,1)}, bf16[256,3,512]{2,0,1:T(8,128)(2,1)S(1)}, u32[]{:S(2)}, u32[]{:S(2)}) collective-permute-start(bf16[256,3,512]{2,0,1:T(8,128)(2,1)} %param.13), channel_id=1, source_target_pairs={{0,12},{4,0},{8,4},{12,8},{1,13},{5,1},{9,5},{13,9},{2,14},{6,2},{... | collective-permute-start | bytes 2359304 | tf_op jit(solution)/shard_map/ppermute | solution.py:16
  57.3 16.0 %all-to-all-start = ((bf16[1,8,128,4]{2,3,0,1:T(4,128)(2,1)}), bf16[1,8,128,4]{2,3,0,1:T(4,128)(2,1)S(1)}, u32[]{:S(2)}, u32[]{:S(2)}) async-start(bf16[1,8,128,4]{2,3,0,1:T(4,128)(2,1)} %bitcast.221), calls=%async_computation | async-start | bytes 16384 | tf_op jit(solution)/shard_map/all_to_all | solution.py:92
  60.6 46.9 %all-gather.4.cloned.1.call-start = ((), (), s32[]{:S(2)}) async-start(), calls=%async_computation.3 | async-start | bytes 3145728 | tf_op jit(solution)/shard_map/all_gather | solution.py:94
  63.7 34.6 %copy-start.1 = (bf16[256,3,512]{2,0,1:T(8,128)(2,1)S(1)}, bf16[256,3,512]{2,0,1:T(8,128)(2,1)}, u32[]{:S(2)}) copy-start(bf16[256,3,512]{2,0,1:T(8,128)(2,1)} %param.13) | copy-start | bytes 2359300
  63.7 127.7 %all-gather.6.cloned.1.call-start = ((), (), s32[]{:S(2)}) async-start(), calls=%async_computation.4 | async-start | bytes 3145728 | tf_op jit(solution)/shard_map/all_gather | solution.py:142
  75.6 20.3 %collective-permute-start.2 = (bf16[256,3,512]{2,0,1:T(8,128)(2,1)}, bf16[256,3,512]{2,0,1:T(8,128)(2,1)}, u32[]{:S(2)}, u32[]{:S(2)}) collective-permute-start(bf16[256,3,512]{2,0,1:T(8,128)(2,1)} %collective-permute-done.1), channel_id=1, source_target_pairs={{0,4},{4,8},{8,12},{12,0},{1,5},{5,9},{9,13},{13,1},{2,6},{6,10},{... | collective-permute-start | bytes 2359304 | tf_op jit(solution)/shard_map/ppermute | solution.py:14
  154.3 5.2 %collective-permute-start = (f32[1,4,128,128]{3,2,1,0:T(8,128)S(1)}, f32[1,4,128,128]{3,2,1,0:T(8,128)S(1)}, u32[]{:S(2)}, u32[]{:S(2)}) collective-permute-start(f32[1,4,128,128]{3,2,1,0:T(8,128)S(1)} %multiply_add_fusion.3), channel_id=1, source_target_pairs={{0,4},{4,8},{8,12},{1,5},{5,9},{9,13},{2,6},{6,10},{10,14},{3,7},{... | collective-permute-start | bytes 786440 | tf_op jit(solution)/shard_map/while/body/eval_jaxpr/ppermute | solution.py:24
  159.5 8.3 %collective-permute-start = (f32[1,4,128,128]{3,2,1,0:T(8,128)S(1)}, f32[1,4,128,128]{3,2,1,0:T(8,128)S(1)}, u32[]{:S(2)}, u32[]{:S(2)}) collective-permute-start(f32[1,4,128,128]{3,2,1,0:T(8,128)S(1)} %multiply_add_fusion.3), channel_id=1, source_target_pairs={{0,4},{4,8},{8,12},{1,5},{5,9},{9,13},{2,6},{6,10},{10,14},{3,7},{... | collective-permute-start | bytes 786440 | tf_op jit(solution)/shard_map/while/body/eval_jaxpr/ppermute | solution.py:24
  167.9 8.3 %collective-permute-start = (f32[1,4,128,128]{3,2,1,0:T(8,128)S(1)}, f32[1,4,128,128]{3,2,1,0:T(8,128)S(1)}, u32[]{:S(2)}, u32[]{:S(2)}) collective-permute-start(f32[1,4,128,128]{3,2,1,0:T(8,128)S(1)} %multiply_add_fusion.3), channel_id=1, source_target_pairs={{0,4},{4,8},{8,12},{1,5},{5,9},{9,13},{2,6},{6,10},{10,14},{3,7},{... | collective-permute-start | bytes 786440 | tf_op jit(solution)/shard_map/while/body/eval_jaxpr/ppermute | solution.py:24
  180.3 60.5 %reduce-scatter.2.cloned.1.call-start = ((), (), s32[]{:S(2)}) async-start(), calls=%async_computation.6 | async-start | bytes 2621440 | tf_op jit(solution)/shard_map/reduce_scatter | solution.py:149
  191.3 78.3 %copy-start.2 = (bf16[1024,1024]{0,1:T(8,128)(2,1)S(1)}, bf16[1024,1024]{0,1:T(8,128)(2,1)}, u32[]{:S(2)}) copy-start(bf16[1024,1024]{0,1:T(8,128)(2,1)} %all-gather.6.cloned.1.call-done) | copy-start | bytes 6291460
  195.7 74.0 %all-gather.8.cloned.1.call-start = ((), (), s32[]{:S(2)}) async-start(), calls=%async_computation.5 | async-start | bytes 1310720 | tf_op jit(solution)/shard_map/all_gather | solution.py:97
  196.2 103.8 %all-reduce.2.cloned.1.call-start = ((), (), s32[]{:S(2)}) async-start(), calls=%async_computation.7 | async-start | bytes 1048576 | tf_op jit(solution)/shard_map/psum | solution.py:158
Sparse Core Ops, SparseCore 0:
  63.8 11.9 all-gather.3
  180.4 10.8 all-gather.5
  195.8 45.0 reduce-scatter.1
  242.4 27.2 all-gather.7
  271.9 28.0 all-reduce.1
